TPU v7x, 32 devices: a whole 2x2x4 slice. The times are simulated.
32 devices in a mesh: groups: 2 (over x), row: 16 (over z, y, core).
Axes of the slice: x: 2, y: 2, z: 4, core: 2. Of those that a mesh axis runs over, the one named last changes fastest.
Arguments:
- enc_dict: bfloat16 [8192, 4096], P('row'), may hold values from -0.09375 to 0.09375
- dec_dict: bfloat16 [8192, 4096], P('row'), may hold values from -0.09375 to 0.09375
- active_ids: int32 [4096], P(('groups', 'row')), parts along dimension 0, may hold values from 0 to 8191, as said below
- counts: int32 [32], P(('groups', 'row')), parts along dimension 0, may hold values from 1 to 128
- strengths: float32 [4096], P(('groups', 'row')), parts along dimension 0, may hold values from 0.25 to 4
- layers: int32 [4096], P(('groups', 'row')), parts along dimension 0, may hold values from 0 to 25
- positions: int32 [4096], P(('groups', 'row')), parts along dimension 0, may hold values from 0 to 127
- targets: float32 [4096, 128], P(('groups', 'row')), parts along dimension 0, may hold values from -6 to 6
Outputs:
- influence: float32 [4096, 128], P(('groups', 'row')), parts along dimension 0
There are 2 independent parts, one for each index of `groups`. A program takes and returns all parts, laid end to end along the dimension named above; an argument that names none is the same for every part. Nothing has to cross between parts.
Inputs may be any that keep to these rules, and one draw needn't show every extreme that they name: `active_ids`: the ids in the d-th block of 128 slots are distinct, increasing, and lie in d * 512 to (d + 1) * 512 - 1.
All inputs are finite; a program needn't handle non-finite values.
Results may differ from a plain program's by a relative error of at most 0.0029.
Values may be sent and summed in bfloat16 or wider, within the bound.
A program may use at most 128 MiB of HBM per device.

v0:
```python
import jax
import jax.numpy as jnp
from jax import lax
from jax.sharding import PartitionSpec as P

FLOOR = 1.0


def swapped(array, axis, stride):
    return lax.ppermute(array, axis, [(i, i ^ 1 << stride) for i in range(lax.axis_size(axis))])


def arrange(mine, other, bit, row_index):
    upper = row_index >> bit & 1 == 1
    return jnp.where(upper, jnp.concatenate([other, mine], 0), jnp.concatenate([mine, other], 0))


def split_half(activation_values, bit, row_index):
    upper = row_index >> bit & 1 == 1
    size = activation_values.shape[0] // 2
    lower_part = activation_values[:size]
    upper_part = activation_values[size:]
    keep = jnp.where(upper, upper_part, lower_part)
    send = jnp.where(upper, lower_part, upper_part)
    return (keep, send)


def members(bit_list, row_index):
    mask = 0
    for bit in bit_list:
        mask = mask | 1 << bit
    spots = jnp.arange(1 << len(bit_list), dtype=jnp.int32)
    devices = jnp.zeros_like(spots) + (row_index & ~mask)
    for order, bit in enumerate(bit_list):
        devices = devices | (spots >> order & 1) << bit
    return devices


def gather_sources(activation_values, bit_list, row_index):
    for bit in bit_list:
        activation_values = arrange(
            activation_values, swapped(activation_values, "row", bit), bit, row_index
        )
    return activation_values


def gather_receivers(activation_values, bit_list, row_index):
    for bit in bit_list:
        activation_values = arrange(
            activation_values, swapped(activation_values, "row", bit), bit, row_index
        )
    return activation_values


def gather_power(activation_values, bit_list, row_index):
    for bit in bit_list:
        activation_values = arrange(
            activation_values, swapped(activation_values, "row", bit), bit, row_index
        )
    return activation_values


def reduce_power(activation_values, bit_list, row_index):
    for bit in reversed(bit_list):
        keep, send = split_half(activation_values, bit, row_index)
        activation_values = keep + swapped(send, "row", bit)
    return activation_values


def per_device(enc_dict, dec_dict, active_ids, counts, strengths, layers, positions, targets):
    bits = lax.axis_size("row").bit_length() - 1
    half = bits // 2
    row_index = lax.axis_index("row")
    row_bits = list(range(half))
    col_bits = list(range(half, bits))
    feat_local = enc_dict.shape[0]
    slots = active_ids.shape[0]
    local = active_ids - row_index * feat_local
    live = jnp.arange(slots, dtype=jnp.int32) < counts[0]
    weight = jnp.where(live, strengths, jnp.float32(0.0))
    sources = (weight[:, None] * dec_dict[local].astype(jnp.float32)).astype(jnp.bfloat16)
    receivers = jnp.where(live[:, None], enc_dict[local], jnp.zeros((), jnp.bfloat16))
    all_layers, all_positions = (
        lax.all_gather(layers, "row", axis=0, tiled=True),
        lax.all_gather(positions, "row", axis=0, tiled=True),
    )
    all_layers = all_layers.reshape(-1, slots)
    all_positions = all_positions.reshape(-1, slots)
    row_devices = members(row_bits, row_index)
    col_devices = members(col_bits, row_index)
    row_layer = all_layers[row_devices].reshape(-1)
    row_pos = all_positions[row_devices].reshape(-1)
    col_layer = all_layers[col_devices].reshape(-1)
    col_pos = all_positions[col_devices].reshape(-1)
    source_block = gather_sources(sources, row_bits, row_index)
    receiver_block = gather_receivers(receivers, col_bits, row_index)
    edge_weights = lax.dot_general(
        source_block, receiver_block, (((1,), (1,)), ((), ())), preferred_element_type=jnp.float32
    )
    keep = (row_layer[:, None] < col_layer[None, :]) & (row_pos[:, None] <= col_pos[None, :])
    edge_weights = jnp.where(keep, edge_weights, jnp.float32(0.0))
    magnitude = jnp.sum(jnp.abs(edge_weights), axis=0)
    for bit in col_bits:
        magnitude = magnitude + swapped(magnitude, "row", bit)
    edge_weights = edge_weights * (1.0 / jnp.maximum(magnitude, jnp.float32(FLOOR)))[None, :]
    own_scale = jnp.ones((slots,), jnp.float32)
    state = targets
    total = jnp.zeros_like(targets)
    for step in range(3):
        inputs = gather_power(own_scale[:, None] * state, col_bits, row_index)
        partial_rows = jnp.dot(
            edge_weights,
            inputs,
            precision=lax.Precision.HIGHEST,
            preferred_element_type=jnp.float32,
        )
        state = reduce_power(partial_rows, row_bits, row_index)
        total = total + state
    return total


def solution(mesh):
    in_specs = (
        P("row", None),
        P("row", None),
        P(("groups", "row")),
        P(("groups", "row")),
        P(("groups", "row")),
        P(("groups", "row")),
        P(("groups", "row")),
        P(("groups", "row"), None),
    )
    out_specs = P(("groups", "row"), None)
    return jax.shard_map(
        per_device, mesh=mesh, in_specs=in_specs, out_specs=out_specs, check_vma=False
    )
```

profile of v0, /device:TPU:0, one launch (start us, length us, event | category | flops | bytes accessed | tf_op | source)
XLA Modules:
  0.0 234.3 jit_solution(1520880687186116949)
XLA Ops:
  0.0 0.7 compare_select_fusion
  1.3 4.9 %gather_fusion.4 = bf16[128,4096]{1,0:T(8,128)(2,1)S(1)} fusion(bf16[512,4096]{1,0:T(8,128)(2,1)} %param.9, s32[1024]{0:T(1024)S(1)} %pad_clamp_fusion), kind=kCustom, calls=%fused_computation.4 | custom fusion | bytes 2097664 | tf_op jit(solution)/shard_map/gather | solution.py:81
  7.1 4.9 %gather_fusion.5 = bf16[128,4096]{1,0:T(8,128)(2,1)S(1)} fusion(bf16[512,4096]{1,0:T(8,128)(2,1)} %param.8, s32[1024]{0:T(1024)S(1)} %pad_clamp_fusion), kind=kCustom, calls=%fused_computation.5 | custom fusion | bytes 2097664 | tf_op jit(solution)/shard_map/gather | solution.py:82
  12.2 2.7 %collective-permute-start.2 = (bf16[128,4096]{1,0:T(8,128)(2,1)S(1)}, bf16[128,4096]{1,0:T(8,128)(2,1)S(1)}, u32[]{:S(2)}, u32[]{:S(2)}) collective-permute-start(bf16[128,4096]{1,0:T(8,128)(2,1)S(1)} %broadcast_select_fusion), channel_id=1, source_target_pairs={{0,4},{1,5},{2,6},{3,7},{4,0},{5,1},{6,2},{7,3},{8,12},{9,13},{10,... | collective-permute-start | bytes 3145736 | tf_op jit(solution)/shard_map/ppermute | solution.py:10
  14.8 3.6 %maximum_select_fusion.4 = bf16[256,4096]{1,0:T(8,128)(2,1)} fusion(bf16[128,4096]{1,0:T(8,128)(2,1)S(1)} %multiply_convert_fusion, bf16[128,4096]{1,0:T(8,128)(2,1)} %collective-permute-done, pred[]{:T(512)S(6)} %eq.8), kind=kLoop, calls=%fused_computation.21 | loop fusion | flops 9437184 | bytes 4194305 | tf_op jit(solution)/shard_map/jit(_where)/select_n | solution.py:15
  18.5 1.5 collective-permute-start.1
  20.0 18.7 %collective-permute-done.2 = bf16[128,4096]{1,0:T(8,128)(2,1)S(1)} collective-permute-done((bf16[128,4096]{1,0:T(8,128)(2,1)S(1)}, bf16[128,4096]{1,0:T(8,128)(2,1)S(1)}, u32[]{:S(2)}, u32[]{:S(2)}) %collective-permute-start.2) | collective-permute-done | bytes 1048608 | tf_op jit(solution)/shard_map/ppermute | solution.py:10
  38.6 1.8 maximum_select_fusion.5
  40.5 2.8 %collective-permute-start.3 = (bf16[256,4096]{1,0:T(8,128)(2,1)}, bf16[256,4096]{1,0:T(8,128)(2,1)S(1)}, u32[]{:S(2)}, u32[]{:S(2)}) collective-permute-start(bf16[256,4096]{1,0:T(8,128)(2,1)} %maximum_select_fusion.5), channel_id=1, source_target_pairs={{0,8},{1,9},{2,10},{3,11},{4,12},{5,13},{6,14},{7,15},{8,0},{9,1},... | collective-permute-start | bytes 6291464 | tf_op jit(solution)/shard_map/ppermute | solution.py:10
  43.2 1.6 collective-permute-start.6
  44.8 60.2 %all-gather = s32[16,1,128]{2,1,0:T(1,128)S(1)} all-gather(s32[1,1,128]{2,1,0:T(1,128)S(1)} %bitcast.35), channel_id=1, replica_groups=mesh['groups'=2,'row'=16] {'row'}, dimensions={0}, use_global_device_ids=true | all-gather | bytes 8704 | tf_op jit(solution)/shard_map/all_gather | solution.py:84
  106.2 59.5 %all-gather.1 = s32[16,1,128]{2,1,0:T(1,128)S(1)} all-gather(s32[1,1,128]{2,1,0:T(1,128)S(1)} %bitcast.36), channel_id=1, replica_groups=mesh['groups'=2,'row'=16] {'row'}, dimensions={0}, use_global_device_ids=true | all-gather | bytes 8704 | tf_op jit(solution)/shard_map/all_gather | solution.py:85
  166.8 6.4 %abs_reduce_fusion = (f32[512]{0:T(512)S(1)}, f32[512,512]{1,0:T(8,128)S(1)}) fusion(s32[512]{0:T(512)S(1)} %bitcast.31, s32[512]{0:T(512)S(1)} %bitcast.27, s32[512]{0:T(512)S(1)} %bitcast.23, s32[512]{0:T(512)S(1)} %bitcast.19, bf16[256,4096]{1,0:T(8,128)(2,1)} %maximum_select_fusion.5, bf16[256,4096]{1,0:T(8,128)(2,1)S(1)} %collective-permute-done.3, ...), kind=kOutput, calls=%fused_computation.24 | convolution fusion | flops 2186804736 | bytes 9447426 | tf_op jit(solution)/shard_map/dot_general | solution.py:97
  173.3 3.6 %collective-permute-done.4 = f32[512]{0:T(512)S(1)} collective-permute-done((f32[512]{0:T(512)S(1)}, f32[512]{0:T(512)S(1)}, u32[]{:S(2)}, u32[]{:S(2)}) %collective-permute-start.4) | collective-permute-done | bytes 2080 | tf_op jit(solution)/shard_map/ppermute | solution.py:10
  176.9 3.0 %collective-permute-start.7 = (f32[256,128]{1,0:T(8,128)S(1)}, f32[256,128]{1,0:T(8,128)S(1)}, u32[]{:S(2)}, u32[]{:S(2)}) collective-permute-start(f32[256,128]{1,0:T(8,128)S(1)} %maximum_select_fusion.12), channel_id=1, source_target_pairs={{0,8},{1,9},{2,10},{3,11},{4,12},{5,13},{6,14},{7,15},{8,0},{9,1},... | collective-permute-start | bytes 393224 | tf_op jit(solution)/shard_map/ppermute | solution.py:10
  179.9 2.4 %collective-permute-done.5 = f32[512]{0:T(512)S(1)} collective-permute-done((f32[512]{0:T(512)S(1)}, f32[512]{0:T(512)S(1)}, u32[]{:S(2)}, u32[]{:S(2)}) %collective-permute-start.5) | collective-permute-done | bytes 2080 | tf_op jit(solution)/shard_map/ppermute | solution.py:10
  182.3 2.7 %collective-permute-done.7 = f32[256,128]{1,0:T(8,128)S(1)} collective-permute-done((f32[256,128]{1,0:T(8,128)S(1)}, f32[256,128]{1,0:T(8,128)S(1)}, u32[]{:S(2)}, u32[]{:S(2)}) %collective-permute-start.7) | collective-permute-done | bytes 131104 | tf_op jit(solution)/shard_map/ppermute | solution.py:10
  185.0 1.1 fusion.17
  186.2 5.4 %collective-permute-done.8 = f32[256,128]{1,0:T(8,128)S(1)} collective-permute-done((f32[256,128]{1,0:T(8,128)S(1)}, f32[256,128]{1,0:T(8,128)S(1)}, u32[]{:S(2)}, u32[]{:S(2)}) %collective-permute-start.8) | collective-permute-done | bytes 131104 | tf_op jit(solution)/shard_map/ppermute | solution.py:10
  191.8 1.2 collective-permute-done.9
  193.1 4.3 %collective-permute-done.10 = f32[128,128]{1,0:T(8,128)S(1)} collective-permute-done((f32[128,128]{1,0:T(8,128)S(1)}, f32[128,128]{1,0:T(8,128)S(1)}, u32[]{:S(2)}, u32[]{:S(2)}) %collective-permute-start.10) | collective-permute-done | bytes 65568 | tf_op jit(solution)/shard_map/ppermute | solution.py:10
  197.4 0.9 collective-permute-start.11
  198.3 7.2 %collective-permute-done.11 = f32[256,128]{1,0:T(8,128)S(1)} collective-permute-done((f32[256,128]{1,0:T(8,128)S(1)}, f32[256,128]{1,0:T(8,128)S(1)}, u32[]{:S(2)}, u32[]{:S(2)}) %collective-permute-start.11) | collective-permute-done | bytes 131104 | tf_op jit(solution)/shard_map/ppermute | solution.py:10
  205.5 1.1 fusion.15
  207.1 4.9 %collective-permute-done.12 = f32[256,128]{1,0:T(8,128)S(1)} collective-permute-done((f32[256,128]{1,0:T(8,128)S(1)}, f32[256,128]{1,0:T(8,128)S(1)}, u32[]{:S(2)}, u32[]{:S(2)}) %collective-permute-start.12) | collective-permute-done | bytes 131104 | tf_op jit(solution)/shard_map/ppermute | solution.py:10
  212.1 1.2 collective-permute-done.13
  213.4 4.3 %collective-permute-done.14 = f32[128,128]{1,0:T(8,128)S(1)} collective-permute-done((f32[128,128]{1,0:T(8,128)S(1)}, f32[128,128]{1,0:T(8,128)S(1)}, u32[]{:S(2)}, u32[]{:S(2)}) %collective-permute-start.14) | collective-permute-done | bytes 65568 | tf_op jit(solution)/shard_map/ppermute | solution.py:10
  217.7 0.9 collective-permute-start.15
  218.5 7.3 %collective-permute-done.15 = f32[256,128]{1,0:T(8,128)S(1)} collective-permute-done((f32[256,128]{1,0:T(8,128)S(1)}, f32[256,128]{1,0:T(8,128)S(1)}, u32[]{:S(2)}, u32[]{:S(2)}) %collective-permute-start.15) | collective-permute-done | bytes 131104 | tf_op jit(solution)/shard_map/ppermute | solution.py:10
  225.9 1.1 fusion.13
  227.4 4.9 %collective-permute-done.16 = f32[256,128]{1,0:T(8,128)S(1)} collective-permute-done((f32[256,128]{1,0:T(8,128)S(1)}, f32[256,128]{1,0:T(8,128)S(1)}, u32[]{:S(2)}, u32[]{:S(2)}) %collective-permute-start.16) | collective-permute-done | bytes 131104 | tf_op jit(solution)/shard_map/ppermute | solution.py:10
  232.4 1.2 collective-permute-done.17
  (53 shorter events, 5.3 us)
Async XLA Ops:
  1.3 5.0 %copy-start.3 = (f32[128]{0:T(128)S(1)}, f32[128]{0:T(128)}, u32[]{:S(2)}) copy-start(f32[128]{0:T(128)} %param.12) | copy-start | bytes 1540
  6.6 8.3 %collective-permute-start = (bf16[128,4096]{1,0:T(8,128)(2,1)S(1)}, bf16[128,4096]{1,0:T(8,128)(2,1)}, u32[]{:S(2)}, u32[]{:S(2)}) collective-permute-start(bf16[128,4096]{1,0:T(8,128)(2,1)S(1)} %multiply_convert_fusion), channel_id=1, source_target_pairs={{0,1},{1,0},{2,3},{3,2},{4,5},{5,4},{6,7},{7,6},{8,9},{9,8},{10,11... | collective-permute-start | bytes 3145736 | tf_op jit(solution)/shard_map/ppermute | solution.py:10
  12.2 26.5 %collective-permute-start.2 = (bf16[128,4096]{1,0:T(8,128)(2,1)S(1)}, bf16[128,4096]{1,0:T(8,128)(2,1)S(1)}, u32[]{:S(2)}, u32[]{:S(2)}) collective-permute-start(bf16[128,4096]{1,0:T(8,128)(2,1)S(1)} %broadcast_select_fusion), channel_id=1, source_target_pairs={{0,4},{1,5},{2,6},{3,7},{4,0},{5,1},{6,2},{7,3},{8,12},{9,13},{10,... | collective-permute-start | bytes 3145736 | tf_op jit(solution)/shard_map/ppermute | solution.py:10
  14.8 28.4 %copy-start = (f32[128,128]{1,0:T(8,128)S(1)}, f32[128,128]{1,0:T(8,128)}, u32[]{:S(2)}) copy-start(f32[128,128]{1,0:T(8,128)} %param.15) | copy-start | bytes 196612
  14.8 30.0 %copy-start.1 = (s32[128]{0:T(128)S(1)}, s32[128]{0:T(128)}, u32[]{:S(2)}) copy-start(s32[128]{0:T(128)} %param.13) | copy-start | bytes 1540
  14.8 91.4 %copy-start.2 = (s32[128]{0:T(128)S(1)}, s32[128]{0:T(128)}, u32[]{:S(2)}) copy-start(s32[128]{0:T(128)} %param.14) | copy-start | bytes 1540
  18.5 148.3 %collective-permute-start.1 = (bf16[256,4096]{1,0:T(8,128)(2,1)}, bf16[256,4096]{1,0:T(8,128)(2,1)}, u32[]{:S(2)}, u32[]{:S(2)}) collective-permute-start(bf16[256,4096]{1,0:T(8,128)(2,1)} %maximum_select_fusion.4), channel_id=1, source_target_pairs={{0,2},{1,3},{2,0},{3,1},{4,6},{5,7},{6,4},{7,5},{8,10},{9,11},{10,... | collective-permute-start | bytes 6291464 | tf_op jit(solution)/shard_map/ppermute | solution.py:10
  40.5 126.3 %collective-permute-start.3 = (bf16[256,4096]{1,0:T(8,128)(2,1)}, bf16[256,4096]{1,0:T(8,128)(2,1)S(1)}, u32[]{:S(2)}, u32[]{:S(2)}) collective-permute-start(bf16[256,4096]{1,0:T(8,128)(2,1)} %maximum_select_fusion.5), channel_id=1, source_target_pairs={{0,8},{1,9},{2,10},{3,11},{4,12},{5,13},{6,14},{7,15},{8,0},{9,1},... | collective-permute-start | bytes 6291464 | tf_op jit(solution)/shard_map/ppermute | solution.py:10
  43.2 133.6 %collective-permute-start.6 = (f32[128,128]{1,0:T(8,128)S(1)}, f32[128,128]{1,0:T(8,128)S(1)}, u32[]{:S(2)}, u32[]{:S(2)}) collective-permute-start(f32[128,128]{1,0:T(8,128)S(1)} %copy-done), channel_id=1, source_target_pairs={{0,4},{1,5},{2,6},{3,7},{4,0},{5,1},{6,2},{7,3},{8,12},{9,13},{10,... | collective-permute-start | bytes 196616 | tf_op jit(solution)/shard_map/ppermute | solution.py:10
  173.2 3.7 %collective-permute-start.4 = (f32[512]{0:T(512)S(1)}, f32[512]{0:T(512)S(1)}, u32[]{:S(2)}, u32[]{:S(2)}) collective-permute-start(f32[512]{0:T(512)S(1)} %get-tuple-element.5), channel_id=1, source_target_pairs={{0,4},{1,5},{2,6},{3,7},{4,0},{5,1},{6,2},{7,3},{8,12},{9,13},{10,... | collective-permute-start | bytes 6152 | tf_op jit(solution)/shard_map/ppermute | solution.py:10
  176.9 5.4 %collective-permute-start.5 = (f32[512]{0:T(512)S(1)}, f32[512]{0:T(512)S(1)}, u32[]{:S(2)}, u32[]{:S(2)}) collective-permute-start(f32[512]{0:T(512)S(1)} %add.67), channel_id=1, source_target_pairs={{0,8},{1,9},{2,10},{3,11},{4,12},{5,13},{6,14},{7,15},{8,0},{9,1},... | collective-permute-start | bytes 6152 | tf_op jit(solution)/shard_map/ppermute | solution.py:10
  176.9 8.1 %collective-permute-start.7 = (f32[256,128]{1,0:T(8,128)S(1)}, f32[256,128]{1,0:T(8,128)S(1)}, u32[]{:S(2)}, u32[]{:S(2)}) collective-permute-start(f32[256,128]{1,0:T(8,128)S(1)} %maximum_select_fusion.12), channel_id=1, source_target_pairs={{0,8},{1,9},{2,10},{3,11},{4,12},{5,13},{6,14},{7,15},{8,0},{9,1},... | collective-permute-start | bytes 393224 | tf_op jit(solution)/shard_map/ppermute | solution.py:10
  186.2 5.5 %collective-permute-start.8 = (f32[256,128]{1,0:T(8,128)S(1)}, f32[256,128]{1,0:T(8,128)S(1)}, u32[]{:S(2)}, u32[]{:S(2)}) collective-permute-start(f32[256,128]{1,0:T(8,128)S(1)} %slice_select_fusion.2), channel_id=1, source_target_pairs={{0,2},{1,3},{2,0},{3,1},{4,6},{5,7},{6,4},{7,5},{8,10},{9,11},{10,... | collective-permute-start | bytes 393224 | tf_op jit(solution)/shard_map/ppermute | solution.py:10
  191.7 1.3 collective-permute-start.9
  193.0 4.3 %collective-permute-start.10 = (f32[128,128]{1,0:T(8,128)S(1)}, f32[128,128]{1,0:T(8,128)S(1)}, u32[]{:S(2)}, u32[]{:S(2)}) collective-permute-start(f32[128,128]{1,0:T(8,128)S(1)} %select_add_fusion.4), channel_id=1, source_target_pairs={{0,4},{1,5},{2,6},{3,7},{4,0},{5,1},{6,2},{7,3},{8,12},{9,13},{10,... | collective-permute-start | bytes 196616 | tf_op jit(solution)/shard_map/ppermute | solution.py:10
  197.4 8.2 %collective-permute-start.11 = (f32[256,128]{1,0:T(8,128)S(1)}, f32[256,128]{1,0:T(8,128)S(1)}, u32[]{:S(2)}, u32[]{:S(2)}) collective-permute-start(f32[256,128]{1,0:T(8,128)S(1)} %maximum_select_fusion.13), channel_id=1, source_target_pairs={{0,8},{1,9},{2,10},{3,11},{4,12},{5,13},{6,14},{7,15},{8,0},{9,1},... | collective-permute-start | bytes 393224 | tf_op jit(solution)/shard_map/ppermute | solution.py:10
  206.7 5.2 %collective-permute-start.12 = (f32[256,128]{1,0:T(8,128)S(1)}, f32[256,128]{1,0:T(8,128)S(1)}, u32[]{:S(2)}, u32[]{:S(2)}) collective-permute-start(f32[256,128]{1,0:T(8,128)S(1)} %slice_select_fusion.1), channel_id=1, source_target_pairs={{0,2},{1,3},{2,0},{3,1},{4,6},{5,7},{6,4},{7,5},{8,10},{9,11},{10,... | collective-permute-start | bytes 393224 | tf_op jit(solution)/shard_map/ppermute | solution.py:10
  212.0 1.3 collective-permute-start.13
  213.3 4.3 %collective-permute-start.14 = (f32[128,128]{1,0:T(8,128)S(1)}, f32[128,128]{1,0:T(8,128)S(1)}, u32[]{:S(2)}, u32[]{:S(2)}) collective-permute-start(f32[128,128]{1,0:T(8,128)S(1)} %select_add_fusion.3), channel_id=1, source_target_pairs={{0,4},{1,5},{2,6},{3,7},{4,0},{5,1},{6,2},{7,3},{8,12},{9,13},{10,... | collective-permute-start | bytes 196616 | tf_op jit(solution)/shard_map/ppermute | solution.py:10
  217.7 8.2 %collective-permute-start.15 = (f32[256,128]{1,0:T(8,128)S(1)}, f32[256,128]{1,0:T(8,128)S(1)}, u32[]{:S(2)}, u32[]{:S(2)}) collective-permute-start(f32[256,128]{1,0:T(8,128)S(1)} %maximum_select_fusion.14), channel_id=1, source_target_pairs={{0,8},{1,9},{2,10},{3,11},{4,12},{5,13},{6,14},{7,15},{8,0},{9,1},... | collective-permute-start | bytes 393224 | tf_op jit(solution)/shard_map/ppermute | solution.py:10
  227.0 5.2 %collective-permute-start.16 = (f32[256,128]{1,0:T(8,128)S(1)}, f32[256,128]{1,0:T(8,128)S(1)}, u32[]{:S(2)}, u32[]{:S(2)}) collective-permute-start(f32[256,128]{1,0:T(8,128)S(1)} %slice_select_fusion), channel_id=1, source_target_pairs={{0,2},{1,3},{2,0},{3,1},{4,6},{5,7},{6,4},{7,5},{8,10},{9,11},{10,... | collective-permute-start | bytes 393224 | tf_op jit(solution)/shard_map/ppermute | solution.py:10
  232.3 1.3 collective-permute-start.17
where the time goes:
time: 235 us; the launch traced here: 234 us
  blocking collectives  120 us (51%)
  waiting for transfers between devices  69.3 us (29%)
  starting transfers between devices  15 us (6%)
  local copies, waits for them, and re-layouts  12.1 us (5%)
  matrix products  9.75 us (4%)
  other arithmetic  7.44 us (3%)
    ppermute x18, waiting for transfers between devices, swapped(): lax.ppermute(array, axis, [(i, i ^ 1 << stride) for i in range(lax.axis_s...  69.3 us
    all_gather x1, blocking collectives, per_device(): lax.all_gather(layers, 'row', axis=0, tiled=True)  60.2 us
    all_gather x1, blocking collectives, per_device(): lax.all_gather(positions, 'row', axis=0, tiled=True)  59.5 us
    ppermute x18, starting transfers between devices, swapped(): lax.ppermute(array, axis, [(i, i ^ 1 << stride) for i in range(lax.axis_s...  15 us
    dot_general x1, matrix products, per_device(): lax.dot_general(source_block, receiver_block, (((1,), (1,)), ((), ())), p...  6.37 us
    select_n x5, other arithmetic, arrange(): jnp.where(upper, jnp.concatenate([other, mine], 0), jnp.concatenate([mine...  5.49 us
    gather x1, local copies, waits for them, and re-layouts, per_device(): dec_dict[local].astype(jnp.float32)  4.94 us
    gather x1, local copies, waits for them, and re-layouts, per_device(): enc_dict[local]  4.93 us
  transfers between devices with their start and end apart: 18, of which 14 were waited for; matrix products, arithmetic and copies ran while one was open for 8% of the time, Pallas kernels for 0%

commit v1 on v0

--- a/solution.py
+++ b/solution.py
@@ -1,6 +1,10 @@
+import functools
+
 import jax
 import jax.numpy as jnp
 from jax import lax
+from jax.experimental import pallas as pl
+from jax.experimental.pallas import tpu as pltpu
 from jax.sharding import PartitionSpec as P
 
 FLOOR = 1.0
@@ -119,6 +123,418 @@
     return total
 
 
+MESH = pl.DeviceIdType.MESH
+CHUNKS = 8
+F32 = jnp.float32
+WIRE = jnp.bfloat16
+
+
+def line_kernel(
+    ids_ref, strength_ref, layer_ref, position_ref, count_ref, target_ref, enc_ref, dec_ref,
+    out_ref,
+    encv, decv, sel, weight, s_buf, r_buf, acc, meta, tbuf, xf, part, total, rs_out, rs_in,
+    x_out, x_in, mag, mag_in, res,
+    enc_sem, dec_sem, s_recv, s_send, c_send, r_recv, r_send, meta_recv, meta_send,
+    t_recv, t_send, mag_sem, rs_send, rs_recv, x_send, x_recv, res_sem,
+):
+    slots = ids_ref.shape[1]
+    feats = enc_ref.shape[0]
+    width = enc_ref.shape[1] // CHUNKS
+    me = lax.axis_index("row")
+    z, yc = me // 4, me % 4
+    y, c = yc // 2, yc % 2
+    half = z // 2
+    is_mid = (z == 1) | (z == 2)
+    inner = jnp.where(is_mid, 1, 0)
+    mid_z, end_z = 1 + half, 3 * half
+    mid_id = mid_z * 4 + yc
+    end_id = end_z * 4 + yc
+    other_mid = (2 - half) * 4 + yc
+    y_peer = z * 4 + (1 - y) * 2 + c
+    c_peer = z * 4 + y * 2 + 1 - c
+    r_dst = jnp.where(is_mid, other_mid, mid_id)
+    s_dst = jnp.where(is_mid, y_peer, mid_id)
+    q_own = half * 2 + inner
+    q_end = half * 2
+    b_own = yc * 2 + inner
+    b_end = yc * 2
+    ny = (1 - y) * 2 + c
+
+    def s_copy(k, b, dst, send):
+        rows = pl.ds(pl.multiple_of(b * slots, slots), slots)
+        return pltpu.make_async_remote_copy(
+            src_ref=s_buf.at[k, rows], dst_ref=s_buf.at[k, rows], send_sem=send.at[k, b],
+            recv_sem=s_recv.at[k, b], device_id={"row": dst}, device_id_type=MESH,
+        )
+
+    def r_copy(k, q, dst):
+        rows = pl.ds(pl.multiple_of(q * slots, slots), slots)
+        return pltpu.make_async_remote_copy(
+            src_ref=r_buf.at[k, rows], dst_ref=r_buf.at[k, rows], send_sem=r_send.at[k, q],
+            recv_sem=r_recv.at[k, q], device_id={"row": dst}, device_id_type=MESH,
+        )
+
+    def meta_copy(slot, which, dst):
+        return pltpu.make_async_remote_copy(
+            src_ref=meta.at[slot], dst_ref=meta.at[slot], send_sem=meta_send.at[which],
+            recv_sem=meta_recv.at[slot], device_id={"row": dst}, device_id_type=MESH,
+        )
+
+    def t_copy(q, which, dst):
+        rows = pl.ds(pl.multiple_of(q * slots, slots), slots)
+        return pltpu.make_async_remote_copy(
+            src_ref=tbuf.at[rows], dst_ref=tbuf.at[rows], send_sem=t_send.at[which],
+            recv_sem=t_recv.at[q], device_id={"row": dst}, device_id_type=MESH,
+        )
+
+    def enc_load(k):
+        cols = pl.ds(pl.multiple_of(k * width, width), width)
+        return pltpu.make_async_copy(enc_ref.at[:, cols], encv.at[k], enc_sem.at[k])
+
+    def dec_load(k):
+        cols = pl.ds(pl.multiple_of(k * width, width), width)
+        return pltpu.make_async_copy(dec_ref.at[:, cols], decv.at[k], dec_sem.at[k])
+
+    for k in range(CHUNKS):
+        enc_load(k).start()
+        dec_load(k).start()
+
+    barrier = pltpu.get_barrier_semaphore()
+    for step in range(1, 16):
+        pl.semaphore_signal(
+            barrier, inc=1, device_id={"row": lax.rem(me + step, 16)}, device_id_type=MESH
+        )
+
+    live = lax.broadcasted_iota(jnp.int32, (1, slots), 1) < count_ref[0]
+    local = jnp.where(live, ids_ref[...] - me * feats, -1)
+    for tile in range(feats // slots):
+        feature = lax.broadcasted_iota(jnp.int32, (slots, slots), 0) + tile * slots
+        hot = jnp.where(feature == local, 1.0, 0.0).astype(F32)
+        sel[:, tile * slots:(tile + 1) * slots] = hot.T.astype(jnp.bfloat16)
+    row = jnp.where(live, strength_ref[...], 0.0)
+    weight[...] = jnp.broadcast_to(row, (slots, slots)).T
+
+    rows8 = lax.broadcasted_iota(jnp.int32, (8, slots), 0)
+    meta[me] = jnp.where(
+        rows8 == 0,
+        jnp.broadcast_to(layer_ref[...], (8, slots)),
+        jnp.broadcast_to(position_ref[...], (8, slots)),
+    ).astype(F32)
+    tbuf[pl.ds(pl.multiple_of(q_own * slots, slots), slots), :] = target_ref[...]
+
+    pl.semaphore_wait(barrier, 15)
+
+    def produce(k, carry):
+        enc_load(k).wait()
+        picked = jnp.dot(sel[...], encv[k], preferred_element_type=F32)
+        r_buf[k, pl.ds(pl.multiple_of(q_own * slots, slots), slots), :] = picked.astype(
+            jnp.bfloat16
+        )
+        r_copy(k, q_own, r_dst).start()
+        dec_load(k).wait()
+        picked = jnp.dot(sel[...], decv[k], preferred_element_type=F32) * weight[:, :1]
+        s_buf[k, pl.ds(pl.multiple_of(b_own * slots, slots), slots), :] = picked.astype(
+            jnp.bfloat16
+        )
+        s_copy(k, b_own, s_dst, s_send).start()
+
+        @pl.when(is_mid)
+        def _():
+            s_copy(k, b_own, c_peer, c_send).start()
+
+        return carry
+
+    lax.fori_loop(0, 2, produce, 0)
+    for which in range(8):
+        @pl.when(me != 4 + which)
+        def _():
+            meta_copy(me, which, 4 + which).start()
+    for which in range(2):
+        @pl.when(z != 1 + which)
+        def _():
+            t_copy(q_own, which, (1 + which) * 4 + yc).start()
+    lax.fori_loop(2, CHUNKS, produce, 0)
+
+    @pl.when(is_mid)
+    def _():
+        acc[...] = jnp.zeros_like(acc)
+
+        def forward(k):
+            r_copy(k, q_end, other_mid).wait_recv()
+            r_copy(k, q_end, other_mid).start()
+            s_copy(k, b_end, y_peer, s_send).wait_recv()
+            s_copy(k, b_end, y_peer, s_send).start()
+            s_copy(k, b_end, c_peer, c_send).start()
+            s_copy(k, ny * 2 + 1, c_peer, c_send).wait_recv()
+            s_copy(k, ny * 2 + 1, c_peer, c_send).start()
+
+        def across(k):
+            s_copy(k, ny * 2, c_peer, c_send).wait_recv()
+            s_copy(k, ny * 2, c_peer, c_send).start()
+
+        def multiply(k):
+            for yy in range(2):
+                for zl in range(2):
+                    s_copy(k, (yy * 2 + 1 - c) * 2 + zl, c_peer, c_send).wait_recv()
+            for zl in range(2):
+                r_copy(k, (1 - half) * 2 + zl, other_mid).wait_recv()
+
+            def tile(i, carry):
+                rows = pl.ds(pl.multiple_of(i * 256, 256), 256)
+                acc[rows, :] += lax.dot_general(
+                    s_buf[k, rows, :], r_buf[k], (((1,), (1,)), ((), ())),
+                    preferred_element_type=F32,
+                )
+                return carry
+
+            lax.fori_loop(0, acc.shape[0] // 256, tile, 0)
+
+        def first(k, carry):
+            forward(k)
+            return carry
+
+        lax.fori_loop(0, CHUNKS // 2, first, 0)
+
+        def second(k, carry):
+            forward(k)
+            j = 2 * (k - CHUNKS // 2)
+
+            @pl.when(j > 0)
+            def _():
+                multiply(j - 2)
+                multiply(j - 1)
+
+            across(j)
+            across(j + 1)
+            return carry
+
+        lax.fori_loop(CHUNKS // 2, CHUNKS, second, 0)
+
+        for z_from in range(4):
+            for d in range(4):
+                slot = z_from * 4 + d
+
+                @pl.when(me != slot)
+                def _():
+                    meta_copy(slot, 0, me).wait_recv()
+        for q in range(4):
+            @pl.when(q_own != q)
+            def _():
+                t_copy(q, 0, me).wait_recv()
+
+        def last(k, carry):
+            multiply(k)
+            return carry
+
+        lax.fori_loop(CHUNKS - 2, CHUNKS, last, 0)
+
+        mag[...] = jnp.zeros_like(mag)
+
+        def mask_rows(b, carry):
+            row_z = jnp.where(b % 2 == 1, mid_z, end_z)
+            info = meta[row_z * 4 + b // 2]
+            row_layer = jnp.broadcast_to(info[0:1], (slots, slots)).T
+            row_pos = jnp.broadcast_to(info[1:2], (slots, slots)).T
+            rows = pl.ds(pl.multiple_of(b * slots, slots), slots)
+            for q, col_z in enumerate((0, 1, 3, 2)):
+                other = meta[col_z * 4 + yc]
+                keep = (row_layer < other[0:1]) & (row_pos <= other[1:2])
+                cols = slice(q * slots, (q + 1) * slots)
+                kept = jnp.where(keep, acc[rows, cols], 0.0)
+                acc[rows, cols] = kept
+                mag[0:1, cols] += jnp.sum(jnp.abs(kept), axis=0, keepdims=True)
+            return carry
+
+        lax.fori_loop(0, 8, mask_rows, 0)
+        mag_copy = pltpu.make_async_remote_copy(
+            src_ref=mag, dst_ref=mag_in, send_sem=mag_sem.at[0], recv_sem=mag_sem.at[1],
+            device_id={"row": other_mid}, device_id_type=MESH,
+        )
+        mag_copy.start()
+        mag_copy.wait()
+        inverse = 1.0 / jnp.maximum(mag[0:1, :] + mag_in[0:1, :], FLOOR)
+
+        def scale(i, carry):
+            rows = pl.ds(pl.multiple_of(i * 64, 64), 64)
+            acc[rows, :] = acc[rows, :] * inverse
+            return carry
+
+        lax.fori_loop(0, acc.shape[0] // 64, scale, 0)
+        xf[...] = tbuf[...]
+        total[...] = jnp.zeros_like(total)
+
+        def rs_copy(t, slot, d, dst):
+            return pltpu.make_async_remote_copy(
+                src_ref=rs_out.at[t, d], dst_ref=rs_in.at[t, slot], send_sem=rs_send.at[t, d],
+                recv_sem=rs_recv.at[t, slot], device_id={"row": dst}, device_id_type=MESH,
+            )
+
+        def x_copy(t):
+            return pltpu.make_async_remote_copy(
+                src_ref=x_out.at[t], dst_ref=x_in.at[t], send_sem=x_send.at[t],
+                recv_sem=x_recv.at[t], device_id={"row": other_mid}, device_id_type=MESH,
+            )
+
+        def power(t, carry):
+            def product(d):
+                rows = pl.ds(pl.multiple_of(d * 2 * slots, 2 * slots), 2 * slots)
+                return jnp.dot(
+                    acc[rows, :], xf[...], precision=lax.Precision.HIGHEST,
+                    preferred_element_type=F32,
+                )
+
+            def send_part(i, carry):
+                d = jnp.where(i == 0, ny, jnp.where(i == 1, (1 - y) * 2 + 1 - c, y * 2 + 1 - c))
+                rs_out[t, d] = product(d).astype(WIRE)
+                rs_copy(t, yc, d, z * 4 + d).start()
+                return carry
+
+            lax.fori_loop(0, 3, send_part, 0)
+            part[...] = product(yc)
+            for d in (ny, (1 - y) * 2 + 1 - c, y * 2 + 1 - c):
+                rs_copy(t, d, d, z * 4 + d).wait_recv()
+                part[...] += rs_in[t, d].astype(F32)
+            total[...] += part[...]
+
+            @pl.when(t < 2)
+            def _():
+                x_out[t] = part[...].astype(WIRE)
+                x_copy(t).start()
+                mine = pl.ds(pl.multiple_of(half * 2 * slots, 2 * slots), 2 * slots)
+                theirs = pl.ds(pl.multiple_of((1 - half) * 2 * slots, 2 * slots), 2 * slots)
+                xf[mine, :] = part[...]
+                x_copy(t).wait_recv()
+                xf[theirs, :] = x_in[t].astype(F32)
+
+            return carry
+
+        lax.fori_loop(0, 3, power, 0)
+
+    res_copy = pltpu.make_async_remote_copy(
+        src_ref=total.at[pl.ds(0, slots)], dst_ref=res, send_sem=res_sem.at[0],
+        recv_sem=res_sem.at[1], device_id={"row": jnp.where(is_mid, end_id, mid_id)},
+        device_id_type=MESH,
+    )
+
+    @pl.when(is_mid)
+    def _():
+        res_copy.start()
+        out_ref[...] = total[slots:2 * slots, :]
+
+        def drain(k, carry):
+            r_copy(k, q_end, other_mid).wait_send()
+            s_copy(k, b_end, y_peer, s_send).wait_send()
+            for b in (b_own, b_end, ny * 2, ny * 2 + 1):
+                s_copy(k, b, c_peer, c_send).wait_send()
+            return carry
+
+        lax.fori_loop(0, CHUNKS, drain, 0)
+
+        def drain_power(t, carry):
+            for d in (ny, (1 - y) * 2 + 1 - c, y * 2 + 1 - c):
+                pltpu.make_async_remote_copy(
+                    src_ref=rs_out.at[t, d], dst_ref=rs_in.at[t, d], send_sem=rs_send.at[t, d],
+                    recv_sem=rs_recv.at[t, d], device_id={"row": z * 4 + d}, device_id_type=MESH,
+                ).wait_send()
+            return carry
+
+        lax.fori_loop(0, 3, drain_power, 0)
+        for t in range(2):
+            pltpu.make_async_remote_copy(
+                src_ref=x_out.at[t], dst_ref=x_in.at[t], send_sem=x_send.at[t],
+                recv_sem=x_recv.at[t], device_id={"row": other_mid}, device_id_type=MESH,
+            ).wait_send()
+        res_copy.wait_send()
+
+    def drain_own(k, carry):
+        r_copy(k, q_own, r_dst).wait_send()
+        s_copy(k, b_own, s_dst, s_send).wait_send()
+        return carry
+
+    lax.fori_loop(0, CHUNKS, drain_own, 0)
+    for which in range(8):
+        @pl.when(me != 4 + which)
+        def _():
+            meta_copy(me, which, 4 + which).wait_send()
+    for which in range(2):
+        @pl.when(z != 1 + which)
+        def _():
+            t_copy(q_own, which, (1 + which) * 4 + yc).wait_send()
+
+    @pl.when(jnp.logical_not(is_mid))
+    def _():
+        res_copy.wait_recv()
+        out_ref[...] = res[...]
+
+
+def per_device_line(enc_dict, dec_dict, active_ids, counts, strengths, layers, positions, targets):
+    slots = active_ids.shape[0]
+    feats, depth = enc_dict.shape
+    width = depth // CHUNKS
+    outs = targets.shape[1]
+    vmem = pl.BlockSpec(memory_space=pltpu.VMEM)
+    dma = pltpu.SemaphoreType.DMA
+    bf16 = jnp.bfloat16
+    return pl.pallas_call(
+        line_kernel,
+        out_shape=jax.ShapeDtypeStruct(targets.shape, F32),
+        in_specs=[vmem] * 4
+        + [pl.BlockSpec(memory_space=pltpu.SMEM), vmem]
+        + [pl.BlockSpec(memory_space=pl.ANY)] * 2,
+        out_specs=vmem,
+        scratch_shapes=[
+            pltpu.VMEM((CHUNKS, feats, width), bf16),
+            pltpu.VMEM((CHUNKS, feats, width), bf16),
+            pltpu.VMEM((slots, feats), bf16),
+            pltpu.VMEM((slots, slots), F32),
+            pltpu.VMEM((CHUNKS, 8 * slots, width), bf16),
+            pltpu.VMEM((CHUNKS, 4 * slots, width), bf16),
+            pltpu.VMEM((8 * slots, 4 * slots), F32),
+            pltpu.VMEM((16, 8, slots), F32),
+            pltpu.VMEM((4 * slots, outs), F32),
+            pltpu.VMEM((4 * slots, outs), F32),
+            pltpu.VMEM((2 * slots, outs), F32),
+            pltpu.VMEM((2 * slots, outs), F32),
+            pltpu.VMEM((3, 4, 2 * slots, outs), WIRE),
+            pltpu.VMEM((3, 4, 2 * slots, outs), WIRE),
+            pltpu.VMEM((2, 2 * slots, outs), WIRE),
+            pltpu.VMEM((2, 2 * slots, outs), WIRE),
+            pltpu.VMEM((8, 4 * slots), F32),
+            pltpu.VMEM((8, 4 * slots), F32),
+            pltpu.VMEM((slots, outs), F32),
+            dma((CHUNKS,)),
+            dma((CHUNKS,)),
+            dma((CHUNKS, 8)),
+            dma((CHUNKS, 8)),
+            dma((CHUNKS, 8)),
+            dma((CHUNKS, 4)),
+            dma((CHUNKS, 4)),
+            dma((16,)),
+            dma((8,)),
+            dma((4,)),
+            dma((2,)),
+            dma((2,)),
+            dma((3, 4)),
+            dma((3, 4)),
+            dma((2,)),
+            dma((2,)),
+            dma((2,)),
+        ],
+        compiler_params=pltpu.CompilerParams(
+            collective_id=0, has_side_effects=True, vmem_limit_bytes=48 * 1024 * 1024
+        ),
+    )(
+        active_ids.reshape(1, slots),
+        strengths.reshape(1, slots),
+        layers.reshape(1, slots),
+        positions.reshape(1, slots),
+        counts,
+        targets,
+        enc_dict,
+        dec_dict,
+    )
+
+
 def solution(mesh):
     in_specs = (
         P("row", None),
@@ -132,5 +548,9 @@
     )
     out_specs = P(("groups", "row"), None)
     return jax.shard_map(
-        per_device, mesh=mesh, in_specs=in_specs, out_specs=out_specs, check_vma=False
+        per_device_line if mesh.shape["row"] == 16 else per_device,
+        mesh=mesh,
+        in_specs=in_specs,
+        out_specs=out_specs,
+        check_vma=False,
     )

time: 235 us -> 102 us (0.43)
  blocking collectives: 120 us -> 0 us
  Pallas kernels: 0 us -> 94.6 us
  waiting for transfers between devices: 69.3 us -> 0 us
  starting transfers between devices: 15 us -> 0 us
  matrix products: 9.75 us -> 0 us
  other arithmetic: 7.44 us -> 0 us
  local copies, waits for them, and re-layouts: 12.1 us -> 6.27 us
    all_gather x2 -> x0, blocking collectives: 120 us -> none  [the longest x1 60.2 us: per_device(): lax.all_gather(layers, 'row', axis=0, tiled=True)]
    pallas_call x0 -> x1, Pallas kernels: none -> 94.6 us  [per_device_line(): pl.pallas_call(line_kernel, out_shape=jax.ShapeDtypeStruct(targets.shape,...]
    ppermute x18 -> x0, waiting for transfers between devices: 69.3 us -> none  [swapped(): lax.ppermute(array, axis, [(i, i ^ 1 << stride) for i in range(lax.axis_s...]
    ppermute x18 -> x0, starting transfers between devices: 15 us -> none  [swapped(): lax.ppermute(array, axis, [(i, i ^ 1 << stride) for i in range(lax.axis_s...]
    gather x6 -> x0, local copies, waits for them, and re-layouts: 12.1 us -> none  [the longest x1 4.94 us: per_device(): dec_dict[local].astype(jnp.float32)]
    dot_general x4 -> x0, matrix products: 9.75 us -> none  [the longest x1 6.37 us: per_device(): lax.dot_general(source_block, receiver_block, (((1,), (1,)), ((), ())), p...]
    select_n x16 -> x0, other arithmetic: 6.39 us -> none  [the longest x5 5.49 us: arrange(): jnp.where(upper, jnp.concatenate([other, mine], 0), jnp.concatenate([mine...]
    unnamed x8 -> x13, local copies, waits for them, and re-layouts: 0.02 us -> 6.27 us
  transfers between devices with their start and end apart: 18 -> 0, of which waited for: 14 -> 0; matrix products, arithmetic and copies ran while one was open for 8% -> 0% of each run, Pallas kernels for 0% -> 0%
where the time goes in v1:
time: 102 us
  Pallas kernels  94.6 us (93%)
  local copies, waits for them, and re-layouts  6.27 us (6%)
    pallas_call x1, Pallas kernels, per_device_line(): pl.pallas_call(line_kernel, out_shape=jax.ShapeDtypeStruct(targets.shape,...  94.6 us
    unnamed x13, local copies, waits for them, and re-layouts  6.27 us

profile of v1, /device:TPU:0, one launch (start us, length us, event | category | flops | bytes accessed | tf_op | source)
XLA Modules:
  0.0 101.6 jit_solution(11604641836884486619)
XLA Ops:
  0.7 0.0 copy-start
  0.7 2.2 %copy-done = bf16[512,4096]{1,0:T(8,128)(2,1)S(1)} copy-done((bf16[512,4096]{1,0:T(8,128)(2,1)S(1)}, bf16[512,4096]{1,0:T(8,128)(2,1)}, u32[]{:S(2)}) %copy-start) | copy-done | bytes 4194328
  2.8 0.0 copy-start.1
  2.8 0.8 copy-done.1
  3.7 0.0 copy-start.2
  3.7 0.7 copy-done.2
  4.3 0.0 copy-start.3
  4.3 0.7 copy-done.3
  5.0 0.0 copy-start.4
  5.0 0.7 copy-done.4
  5.6 0.0 copy-start.5
  5.7 0.7 copy-done.5
  6.3 94.6 %shard_map.82 = f32[128,128]{1,0:T(8,128)S(1)} custom-call(s32[1,128]{1,0:T(1,128)S(1)} %bitcast.4, f32[1,128]{1,0:T(1,128)S(1)} %bitcast.5, s32[1,128]{1,0:T(1,128)S(1)} %bitcast.6, s32[1,128]{1,0:T(1,128)S(1)} %bitcast.7, s32[1]{0:T(128)S(6)} %copy.10.count_ref, f32[128,128]{1,0:T(8,128)S(1)} %copy-done.1, bf16[512,4096]{1,0:T(8,128)(2,1)S(1)} %copy-done, ...), custom_call_target="tpu_custom_call" | custom-call | tf_op jit(solution)/shard_map/pallas_call | solution.py:478
  100.9 0.6 copy.11
Async XLA Ops:
  0.7 2.2 %copy-start = (bf16[512,4096]{1,0:T(8,128)(2,1)S(1)}, bf16[512,4096]{1,0:T(8,128)(2,1)}, u32[]{:S(2)}) copy-start(bf16[512,4096]{1,0:T(8,128)(2,1)} %enc_ref.1) | copy-start | bytes 12582916
  2.8 0.8 copy-start.1
  3.7 0.7 copy-start.2
  4.3 0.7 copy-start.3
  5.0 0.7 copy-start.4
  5.6 0.7 copy-start.5

commit v2 on v1

--- a/solution.py
+++ b/solution.py
@@ -130,14 +130,14 @@
 
 
 def line_kernel(
-    ids_ref, strength_ref, layer_ref, position_ref, count_ref, target_ref, enc_ref, dec_ref,
+    ids_hbm, strength_hbm, layer_hbm, position_hbm, count_ref, target_hbm, enc_ref, dec_ref,
     out_ref,
-    encv, decv, sel, weight, s_buf, r_buf, acc, meta, tbuf, xf, part, total, rs_out, rs_in,
-    x_out, x_in, mag, mag_in, res,
-    enc_sem, dec_sem, s_recv, s_send, c_send, r_recv, r_send, meta_recv, meta_send,
+    ids_ref, strength_ref, layer_ref, position_ref, encv, decv, sel, weight, s_buf, r_buf, acc, meta, tbuf, xf, part, total, rs_out, rs_in,
+    x_out, x_in, mag, mag_in, res, a_hi, a_lo, x_two,
+    small_sem, enc_sem, dec_sem, s_recv, s_send, c_send, r_recv, r_send, meta_recv, meta_send,
     t_recv, t_send, mag_sem, rs_send, rs_recv, x_send, x_recv, res_sem,
 ):
-    slots = ids_ref.shape[1]
+    slots = ids_hbm.shape[1]
     feats = enc_ref.shape[0]
     width = enc_ref.shape[1] // CHUNKS
     me = lax.axis_index("row")
@@ -195,6 +195,16 @@
         cols = pl.ds(pl.multiple_of(k * width, width), width)
         return pltpu.make_async_copy(dec_ref.at[:, cols], decv.at[k], dec_sem.at[k])
 
+    own = pl.ds(pl.multiple_of(q_own * slots, slots), slots)
+    small = [
+        pltpu.make_async_copy(source, place, small_sem.at[i])
+        for i, (source, place) in enumerate((
+            (ids_hbm, ids_ref), (strength_hbm, strength_ref), (layer_hbm, layer_ref),
+            (position_hbm, position_ref), (target_hbm, tbuf.at[own]),
+        ))
+    ]
+    for copy in small:
+        copy.start()
     for k in range(CHUNKS):
         enc_load(k).start()
         dec_load(k).start()
@@ -205,6 +215,8 @@
             barrier, inc=1, device_id={"row": lax.rem(me + step, 16)}, device_id_type=MESH
         )
 
+    for copy in small:
+        copy.wait()
     live = lax.broadcasted_iota(jnp.int32, (1, slots), 1) < count_ref[0]
     local = jnp.where(live, ids_ref[...] - me * feats, -1)
     for tile in range(feats // slots):
@@ -220,7 +232,6 @@
         jnp.broadcast_to(layer_ref[...], (8, slots)),
         jnp.broadcast_to(position_ref[...], (8, slots)),
     ).astype(F32)
-    tbuf[pl.ds(pl.multiple_of(q_own * slots, slots), slots), :] = target_ref[...]
 
     pl.semaphore_wait(barrier, 15)
 
@@ -356,7 +367,10 @@
 
         def scale(i, carry):
             rows = pl.ds(pl.multiple_of(i * 64, 64), 64)
-            acc[rows, :] = acc[rows, :] * inverse
+            scaled = acc[rows, :] * inverse
+            high = scaled.astype(jnp.bfloat16)
+            a_hi[rows, :] = high
+            a_lo[rows, :] = (scaled - high.astype(F32)).astype(jnp.bfloat16)
             return carry
 
         lax.fori_loop(0, acc.shape[0] // 64, scale, 0)
@@ -375,13 +389,18 @@
                 recv_sem=x_recv.at[t], device_id={"row": other_mid}, device_id_type=MESH,
             )
 
+        outs = xf.shape[1]
+
         def power(t, carry):
+            high = xf[...].astype(jnp.bfloat16)
+            x_two[:, :outs] = high
+            x_two[:, outs:] = (xf[...] - high.astype(F32)).astype(jnp.bfloat16)
+
             def product(d):
                 rows = pl.ds(pl.multiple_of(d * 2 * slots, 2 * slots), 2 * slots)
-                return jnp.dot(
-                    acc[rows, :], xf[...], precision=lax.Precision.HIGHEST,
-                    preferred_element_type=F32,
-                )
+                two = jnp.dot(a_hi[rows, :], x_two[...], preferred_element_type=F32)
+                low = jnp.dot(a_lo[rows, :], x_two[:, :outs], preferred_element_type=F32)
+                return two[:, :outs] + (two[:, outs:] + low)
 
             def send_part(i, carry):
                 d = jnp.where(i == 0, ny, jnp.where(i == 1, (1 - y) * 2 + 1 - c, y * 2 + 1 - c))
@@ -472,17 +491,20 @@
     feats, depth = enc_dict.shape
     width = depth // CHUNKS
     outs = targets.shape[1]
+    hbm = pl.BlockSpec(memory_space=pltpu.HBM)
     vmem = pl.BlockSpec(memory_space=pltpu.VMEM)
     dma = pltpu.SemaphoreType.DMA
     bf16 = jnp.bfloat16
     return pl.pallas_call(
         line_kernel,
         out_shape=jax.ShapeDtypeStruct(targets.shape, F32),
-        in_specs=[vmem] * 4
-        + [pl.BlockSpec(memory_space=pltpu.SMEM), vmem]
-        + [pl.BlockSpec(memory_space=pl.ANY)] * 2,
+        in_specs=[hbm] * 4 + [pl.BlockSpec(memory_space=pltpu.SMEM)] + [hbm] * 3,
         out_specs=vmem,
         scratch_shapes=[
+            pltpu.VMEM((1, slots), jnp.int32),
+            pltpu.VMEM((1, slots), F32),
+            pltpu.VMEM((1, slots), jnp.int32),
+            pltpu.VMEM((1, slots), jnp.int32),
             pltpu.VMEM((CHUNKS, feats, width), bf16),
             pltpu.VMEM((CHUNKS, feats, width), bf16),
             pltpu.VMEM((slots, feats), bf16),
@@ -502,6 +524,10 @@
             pltpu.VMEM((8, 4 * slots), F32),
             pltpu.VMEM((8, 4 * slots), F32),
             pltpu.VMEM((slots, outs), F32),
+            pltpu.VMEM((8 * slots, 4 * slots), bf16),
+            pltpu.VMEM((8 * slots, 4 * slots), bf16),
+            pltpu.VMEM((4 * slots, 2 * outs), bf16),
+            dma((5,)),
             dma((CHUNKS,)),
             dma((CHUNKS,)),
             dma((CHUNKS, 8)),
@@ -521,7 +547,7 @@
             dma((2,)),
         ],
         compiler_params=pltpu.CompilerParams(
-            collective_id=0, has_side_effects=True, vmem_limit_bytes=48 * 1024 * 1024
+            collective_id=0, has_side_effects=True, vmem_limit_bytes=60 * 1024 * 1024
         ),
     )(
         active_ids.reshape(1, slots),

time: 102 us -> 98.1 us (0.962)
  local copies, waits for them, and re-layouts: 6.27 us -> 1.47 us
  Pallas kernels: 94.6 us -> 95.8 us
    unnamed x13 -> x1, local copies, waits for them, and re-layouts: 6.27 us -> 1.47 us
    pallas_call x1, Pallas kernels: 94.6 us -> 95.8 us  [per_device_line(): pl.pallas_call(line_kernel, out_shape=jax.ShapeDtypeStruct(targets.shape,...]
where the time goes in v2:
time: 98.1 us; the launch traced here: 97.9 us
  Pallas kernels  95.8 us (98%)
  local copies, waits for them, and re-layouts  1.47 us (1%)
    pallas_call x1, Pallas kernels, per_device_line(): pl.pallas_call(line_kernel, out_shape=jax.ShapeDtypeStruct(targets.shape,...  95.8 us

profile of v2, /device:TPU:0, one launch (start us, length us, event | category | flops | bytes accessed | tf_op | source)
XLA Modules:
  0.0 97.9 jit_solution(4101750041621543360)
XLA Ops:
  0.7 95.8 %shard_map.82 = f32[128,128]{1,0:T(8,128)} custom-call(s32[1,128]{1,0:T(1,128)} %bitcast.4, f32[1,128]{1,0:T(1,128)} %bitcast.5, s32[1,128]{1,0:T(1,128)} %bitcast.6, s32[1,128]{1,0:T(1,128)} %bitcast.7, s32[1]{0:T(128)S(6)} %copy.10.count_ref, f32[128,128]{1,0:T(8,128)} %target_hbm.1, bf16[512,4096]{1,0:T(8,128)(2,1)} %enc_ref.1, bf16[512,4096]{1,0:T(8,128)(2,1)} %dec_ref.1), custom_call_target="tpu_custom_call" | custom-call | tf_op jit(solution)/shard_map/pallas_call | solution.py:498
  96.5 1.5 %copy.11 = f32[128,128]{1,0:T(8,128)} copy(f32[128,128]{1,0:T(8,128)} %shard_map.82) | data formatting | bytes 131072

commit v3 on v2

--- a/solution.py
+++ b/solution.py
@@ -206,8 +206,8 @@
     for copy in small:
         copy.start()
     for k in range(CHUNKS):
+        dec_load(k).start()
         enc_load(k).start()
-        dec_load(k).start()
 
     barrier = pltpu.get_barrier_semaphore()
     for step in range(1, 16):
@@ -236,19 +236,19 @@
     pl.semaphore_wait(barrier, 15)
 
     def produce(k, carry):
+        dec_load(k).wait()
+        picked = jnp.dot(sel[...], decv[k], preferred_element_type=F32) * weight[:, :1]
+        s_buf[k, pl.ds(pl.multiple_of(b_own * slots, slots), slots), :] = picked.astype(
+            jnp.bfloat16
+        )
+        s_copy(k, b_own, s_dst, s_send).start()
+
         enc_load(k).wait()
         picked = jnp.dot(sel[...], encv[k], preferred_element_type=F32)
         r_buf[k, pl.ds(pl.multiple_of(q_own * slots, slots), slots), :] = picked.astype(
             jnp.bfloat16
         )
         r_copy(k, q_own, r_dst).start()
-        dec_load(k).wait()
-        picked = jnp.dot(sel[...], decv[k], preferred_element_type=F32) * weight[:, :1]
-        s_buf[k, pl.ds(pl.multiple_of(b_own * slots, slots), slots), :] = picked.astype(
-            jnp.bfloat16
-        )
-        s_copy(k, b_own, s_dst, s_send).start()
-
         @pl.when(is_mid)
         def _():
             s_copy(k, b_own, c_peer, c_send).start()
@@ -271,11 +271,11 @@
         acc[...] = jnp.zeros_like(acc)
 
         def forward(k):
-            r_copy(k, q_end, other_mid).wait_recv()
-            r_copy(k, q_end, other_mid).start()
             s_copy(k, b_end, y_peer, s_send).wait_recv()
             s_copy(k, b_end, y_peer, s_send).start()
             s_copy(k, b_end, c_peer, c_send).start()
+            r_copy(k, q_end, other_mid).wait_recv()
+            r_copy(k, q_end, other_mid).start()
             s_copy(k, ny * 2 + 1, c_peer, c_send).wait_recv()
             s_copy(k, ny * 2 + 1, c_peer, c_send).start()
 

time: 98.1 us -> 97.5 us (level)
  no operation moved by 1% of the time
where the time goes in v3:
time: 97.5 us; the launch traced here: 97.3 us
  Pallas kernels  95.2 us (98%)
  local copies, waits for them, and re-layouts  1.47 us (2%)
    pallas_call x1, Pallas kernels, per_device_line(): pl.pallas_call(line_kernel, out_shape=jax.ShapeDtypeStruct(targets.shape,...  95.2 us

profile of v3, /device:TPU:0, one launch (start us, length us, event | category | flops | bytes accessed | tf_op | source)
XLA Modules:
  0.0 97.3 jit_solution(11458617095409554906)
XLA Ops:
  0.7 95.2 %shard_map.82 = f32[128,128]{1,0:T(8,128)} custom-call(s32[1,128]{1,0:T(1,128)} %bitcast.4, f32[1,128]{1,0:T(1,128)} %bitcast.5, s32[1,128]{1,0:T(1,128)} %bitcast.6, s32[1,128]{1,0:T(1,128)} %bitcast.7, s32[1]{0:T(128)S(6)} %copy.10.count_ref, f32[128,128]{1,0:T(8,128)} %target_hbm.1, bf16[512,4096]{1,0:T(8,128)(2,1)} %enc_ref.1, bf16[512,4096]{1,0:T(8,128)(2,1)} %dec_ref.1), custom_call_target="tpu_custom_call" | custom-call | tf_op jit(solution)/shard_map/pallas_call | solution.py:498
  95.9 1.5 %copy.11 = f32[128,128]{1,0:T(8,128)} copy(f32[128,128]{1,0:T(8,128)} %shard_map.82) | data formatting | bytes 131072
